TPU v7x, 256 devices: a whole 4x4x8 slice. The times are simulated.
256 devices in a mesh: seq: 64 (over x, z, core), head: 4 (over y).
Axes of the slice: x: 4, y: 4, z: 8, core: 2. Of those that a mesh axis runs over, the one named last changes fastest.
Arguments:
- queries: bfloat16 [24576, 2048], P('seq', 'head'), may hold values from -120 to 120
- keys: bfloat16 [24576, 2048], P('seq', 'head'), may hold values from -5 to 5
- values: bfloat16 [24576, 2048], P('seq', 'head'), may hold values from -5 to 5
- directions: bfloat16 [24576, 2048], P('seq', 'head'), may hold values from -5 to 5
- beta_logit: float32 [16, 24576], P('head', 'seq'), may hold values from -3 to 7
- out_weight: bfloat16 [2048, 2048], P('head'), may hold values from -0.1875 to 0.1875
Outputs:
- mixed: bfloat16 [24576, 2048], P('seq', 'head')
All inputs are finite; a program needn't handle non-finite values.
Results may differ from a plain program's by a relative error of at most 0.015.
Values may be sent and summed in bfloat16 or wider, within the bound.
A program may use at most 64 MiB of HBM per device.

v0:
```python
import math

import jax
import jax.numpy as jnp
from jax import lax
from jax.sharding import PartitionSpec as P

SUB = 128
WINDOW = 4


highest = lax.Precision.HIGHEST


def shifted(block, axis, distance):
    devices = range(lax.axis_size(axis))
    route = [(i - distance, i) for i in devices if i - distance in devices]
    return lax.ppermute(block, axis, route)


def cut_along(shard, dim, count):
    lengths = shard.shape
    tiles = shard.reshape(*lengths[:dim], count, lengths[dim] // count, *lengths[dim + 1 :])
    return jnp.moveaxis(tiles, dim, 0)


def summed_on_arrival(shard, axis, dim):
    count = lax.axis_size(axis)
    tiles = lax.all_to_all(cut_along(shard, dim, count), axis, 0, 0, tiled=True)
    return jnp.sum(tiles.astype(jnp.float32), axis=0)


def product(pattern, first_op, second_op):
    return jnp.einsum(pattern, first_op, second_op, precision=highest)


def solve_unit(matrix):
    identity_run = jnp.eye(matrix.shape[0], dtype=matrix.dtype)
    return jax.scipy.linalg.solve_triangular(matrix, identity_run, lower=True, unit_diagonal=True)


def block_local(query_rows, key_rows, direction_rows, logits, run_size):
    head_count, length, head_size = query_rows.shape
    run_count = length // run_size
    shape_runs = (head_count, run_count, run_size, head_size)
    queries32 = query_rows.astype(jnp.float32).reshape(shape_runs)
    keys32 = key_rows.astype(jnp.float32).reshape(shape_runs)
    raw_dirs = direction_rows.astype(jnp.float32)
    unit_dirs = (
        raw_dirs * lax.rsqrt(jnp.sum(raw_dirs * raw_dirs, axis=-1, keepdims=True) + 1e-06)
    ).reshape(shape_runs)
    betas = (2.0 * jax.nn.sigmoid(logits)).reshape(head_count, run_count, run_size)
    ones_run = jnp.ones((run_size, run_size), jnp.float32)
    strict_lower = jnp.tril(ones_run, -1)
    inclusive = jnp.tril(ones_run, 0)
    strict_upper = jnp.triu(ones_run, 1)
    identity_run = jnp.eye(run_size, dtype=jnp.float32)
    grams = product("hnce,hnde->hncd", unit_dirs, unit_dirs)
    system = identity_run + grams * strict_lower * betas[:, :, None, :]
    inverse = jax.vmap(solve_unit)(system.reshape(-1, run_size, run_size)).reshape(system.shape)
    coeffs = betas[:, :, :, None] * inverse
    coeff_dirs = product("hnac,hncd->hnad", coeffs, unit_dirs)
    coeff_back = product("hnca,hncd->hnad", coeffs, unit_dirs)
    identity_head = jnp.eye(head_size, dtype=jnp.float32)
    run_maps = identity_head - product("hncd,hnce->hnde", unit_dirs, coeff_dirs)
    query_dirs = product("hnid,hnad->hnia", queries32, unit_dirs) * inclusive
    query_start = queries32 - product("hnia,hnad->hnid", query_dirs, coeff_dirs)
    key_dirs = product("hnjd,hncd->hnjc", keys32, unit_dirs) * strict_upper
    key_end = keys32 - product("hnjc,hncd->hnjd", key_dirs, coeff_back)
    mixed_dirs = product("hnac,hnjc->hnaj", coeffs, key_dirs)
    inside = product("hnid,hnjd->hnij", queries32, keys32) - product(
        "hnia,hnaj->hnij", query_dirs, mixed_dirs
    )
    inside = jnp.where(inclusive > 0, inside, -jnp.inf)
    carried = jnp.zeros((head_count, length, head_size), jnp.float32)
    prefix = jnp.broadcast_to(identity_head, (head_count, head_size, head_size))
    row_parts = []
    query_parts = []
    for index_run in range(run_count):
        starts = query_start[:, index_run]
        query_parts.append(product("hid,hde->hie", starts, prefix))
        across = product("hid,hjd->hij", starts, carried)
        before = index_run * run_size
        after = length - before - run_size
        filler = jnp.full((head_count, run_size, after), -jnp.inf, jnp.float32)
        row_parts.append(
            jnp.concatenate([across[:, :, :before], inside[:, index_run], filler], axis=2)
        )
        carried = product("hjd,hed->hje", carried, run_maps[:, index_run])
        carried = lax.dynamic_update_slice_in_dim(carried, key_end[:, index_run], before, 1)
        prefix = product("hde,hef->hdf", run_maps[:, index_run], prefix)
    own_scores = jnp.concatenate(row_parts, axis=1)
    query_block = jnp.concatenate(query_parts, axis=1)
    return (own_scores, query_block, carried, prefix)


def attend(score_parts, value_parts, head_size):
    scores = jnp.concatenate(score_parts, axis=2) * (1.0 / math.sqrt(head_size))
    maxima = jnp.max(scores, axis=2, keepdims=True)
    weights = jnp.exp(scores - maxima)
    totals = jnp.sum(weights, axis=2, keepdims=True)
    rounded = weights.astype(jnp.bfloat16)
    values_all = jnp.concatenate(value_parts, axis=1)
    attended = jnp.einsum("hik,hkd->hid", rounded, values_all, preferred_element_type=jnp.float32)
    return (attended / totals).astype(jnp.bfloat16)


def per_device(queries, keys, values, directions, beta_logit, out_weight):
    length = queries.shape[0]
    head_count = beta_logit.shape[0]
    head_size = queries.shape[1] // head_count

    def split_heads(array):
        return array.reshape(length, head_count, head_size).transpose(1, 0, 2)

    query_rows = split_heads(queries)
    key_rows = split_heads(keys)
    value_rows = split_heads(values)
    direction_rows = split_heads(directions)
    own_scores, query_block, key_block, block_map = block_local(
        query_rows, key_rows, direction_rows, beta_logit, SUB
    )
    position = lax.axis_index("seq")
    score_parts = [own_scores]
    value_parts = [value_rows]
    carried = lax.optimization_barrier(key_block.astype(jnp.bfloat16)).astype(jnp.float32)
    moving_values = value_rows
    for distance in range(1, WINDOW + 1):
        carried = shifted(carried.astype(jnp.bfloat16), "seq", 1).astype(carried.dtype)
        moving_values = shifted(moving_values, "seq", 1)
        remote = product("hid,hjd->hij", query_block, carried)
        score_parts.append(jnp.where(position >= distance, remote, -jnp.inf))
        value_parts.append(moving_values)
        if distance < WINDOW:
            carried = product("hjd,hed->hje", carried, block_map)
    attended = attend(score_parts, value_parts, head_size)
    attn_rows = attended.transpose(1, 0, 2).reshape(length, head_count * head_size)
    partial_value = jnp.dot(attn_rows, out_weight, preferred_element_type=jnp.float32)
    return summed_on_arrival(partial_value.astype(jnp.bfloat16), "head", 1).astype(jnp.bfloat16)


def solution(mesh):
    return jax.shard_map(
        per_device,
        mesh=mesh,
        in_specs=(
            P("seq", "head"),
            P("seq", "head"),
            P("seq", "head"),
            P("seq", "head"),
            P("head", "seq"),
            P("head", None),
        ),
        out_specs=P("seq", "head"),
        check_vma=False,
    )
```

profile of v0, /device:TPU:1, one launch (start us, length us, event | category | flops | bytes accessed | tf_op | source)
XLA Modules:
  0.0 254.2 jit_solution(7917992333949716470)
XLA Ops:
  6.7 119.8 %custom-call.4 = f32[12,1,128,128]{2,3,1,0:T(8,128)} custom-call(f32[12,1,128,128]{3,2,1,0:T(8,128)} %select_add_fusion), custom_call_target="InvertDiagBlocksLowerTriangular" | custom-call | tf_op jit(solution)/shard_map/vmap(jit(_solve_triangular))/triangular_solve | solution.py:39
  126.4 2.5 fusion.23
  144.3 4.9 %collective-permute-start = (bf16[4,384,128]{2,1,0:T(8,128)(2,1)}, bf16[4,384,128]{2,1,0:T(8,128)(2,1)}, u32[]{:S(2)}, u32[]{:S(2)}) collective-permute-start(bf16[4,384,128]{2,1,0:T(8,128)(2,1)} %fusion.43), channel_id=1, source_target_pairs={{0,4},{4,8},{8,12},{12,16},{16,20},{20,24},{24,28},{28,32},{32,36}... | collective-permute-start | bytes 1179656 | tf_op jit(solution)/shard_map/ppermute | solution.py:18
  151.1 2.2 collective-permute-start.4
  153.4 2.0 fusion.50
  155.4 3.7 %fusion.33 = f32[4,3,128,128]{2,3,1,0:T(8,128)} fusion(f32[4,3,128,128]{2,3,1,0:T(8,128)} %copy-done.8, f32[4,3,128,128]{2,3,1,0:T(8,128)} %bitcast.146, f32[4,3,128]{2,1,0:T(4,128)S(1)} %copy.80), kind=kOutput, calls=%fused_computation.50 | convolution fusion | flops 302186496 | bytes 2365440 | tf_op jit(solution)/shard_map/hnac,hnjc->hnaj/dot_general | solution.py:34
  160.6 2.0 fusion.9
  162.7 2.5 convolution_subtract_fusion.3
  165.2 2.5 fusion.47
  179.8 3.9 %collective-permute-start.1 = (bf16[4,384,128]{2,1,0:T(8,128)(2,1)S(1)}, bf16[4,384,128]{2,1,0:T(8,128)(2,1)S(1)}, u32[]{:S(2)}, u32[]{:S(2)}) collective-permute-start(bf16[4,384,128]{2,1,0:T(8,128)(2,1)S(1)} %convolution_convert_fusion.3), channel_id=1, source_target_pairs={{0,4},{4,8},{8,12},{12,16},{16,20},{20,24},{24,28},{28,32},{32,36}... | collective-permute-start | bytes 1179656 | tf_op jit(solution)/shard_map/ppermute | solution.py:18
  183.8 1.9 collective-permute-start.5
  185.7 3.5 %select_dynamic-update-slice_fusion.3 = f32[4,384,1920]{1,2,0:T(8,128)} fusion(f32[4,384,1920]{1,2,0:T(8,128)} %fusion.7, bf16[4,384,128]{2,1,0:T(8,128)(2,1)} %collective-permute-done, pred[]{:T(512)S(6)} %ge.36, f32[4,128,128]{2,1,0:T(8,128)S(1)} %fusion.49, f32[4,128,128]{2,1,0:T(8,128)S(1)} %fusion.46, f32[4,128,128]{2,1,0:T(8,128)S(1)} %fusion.44), kind=kOutput, calls=%fused_computation.15 | convolution fusion | flops 906952704 | bytes 3538945 | tf_op jit(solution)/shard_map/hid,hjd->hij/dot_general | solution.py:34
  190.8 3.9 %collective-permute-start.2 = (bf16[4,384,128]{2,1,0:T(8,128)(2,1)S(1)}, bf16[4,384,128]{2,1,0:T(8,128)(2,1)S(1)}, u32[]{:S(2)}, u32[]{:S(2)}) collective-permute-start(bf16[4,384,128]{2,1,0:T(8,128)(2,1)S(1)} %convolution_convert_fusion.2), channel_id=1, source_target_pairs={{0,4},{4,8},{8,12},{12,16},{16,20},{20,24},{24,28},{28,32},{32,36}... | collective-permute-start | bytes 1179656 | tf_op jit(solution)/shard_map/ppermute | solution.py:18
  194.7 2.5 %collective-permute-start.6 = (bf16[4,384,128]{1,2,0:T(8,128)(2,1)S(1)}, bf16[4,384,128]{1,2,0:T(8,128)(2,1)S(1)}, u32[]{:S(2)}, u32[]{:S(2)}) collective-permute-start(bf16[4,384,128]{1,2,0:T(8,128)(2,1)S(1)} %collective-permute-done.5), channel_id=1, source_target_pairs={{0,4},{4,8},{8,12},{12,16},{16,20},{20,24},{24,28},{28,32},{32,36}... | collective-permute-start | bytes 1179656 | tf_op jit(solution)/shard_map/ppermute | solution.py:18
  197.3 2.6 %select_dynamic-update-slice_fusion.2 = f32[4,384,1920]{1,2,0:T(8,128)} fusion(f32[4,384,1920]{1,2,0:T(8,128)} %select_dynamic-update-slice_fusion.3, bf16[4,384,128]{2,1,0:T(8,128)(2,1)S(1)} %collective-permute-done.1, pred[]{:T(512)S(6)} %ge.37, f32[4,128,128]{2,1,0:T(8,128)S(1)} %fusion.49, f32[4,128,128]{2,1,0:T(8,128)S(1)} %fusion.46, ...), kind=kOutput, calls=%fused_computation.14 | convolution fusion | flops 906952704 | bytes 3538945 | tf_op jit(solution)/shard_map/hid,hjd->hij/dot_general | solution.py:34
  200.4 4.7 %collective-permute-start.3 = (bf16[4,384,128]{2,1,0:T(8,128)(2,1)S(1)}, bf16[4,384,128]{2,1,0:T(8,128)(2,1)S(1)}, u32[]{:S(2)}, u32[]{:S(2)}) collective-permute-start(bf16[4,384,128]{2,1,0:T(8,128)(2,1)S(1)} %convolution_convert_fusion.1), channel_id=1, source_target_pairs={{0,4},{4,8},{8,12},{12,16},{16,20},{20,24},{24,28},{28,32},{32,36}... | collective-permute-start | bytes 1179656 | tf_op jit(solution)/shard_map/ppermute | solution.py:18
  205.2 2.9 %collective-permute-start.7 = (bf16[4,384,128]{1,2,0:T(8,128)(2,1)S(1)}, bf16[4,384,128]{1,2,0:T(8,128)(2,1)S(1)}, u32[]{:S(2)}, u32[]{:S(2)}) collective-permute-start(bf16[4,384,128]{1,2,0:T(8,128)(2,1)S(1)} %collective-permute-done.6), channel_id=1, source_target_pairs={{0,4},{4,8},{8,12},{12,16},{16,20},{20,24},{24,28},{28,32},{32,36}... | collective-permute-start | bytes 1179656 | tf_op jit(solution)/shard_map/ppermute | solution.py:18
  208.1 2.5 %select_dynamic-update-slice_fusion.1 = f32[4,384,1920]{1,2,0:T(8,128)} fusion(f32[4,384,1920]{1,2,0:T(8,128)} %select_dynamic-update-slice_fusion.2, bf16[4,384,128]{2,1,0:T(8,128)(2,1)S(1)} %collective-permute-done.2, pred[]{:T(512)S(6)} %ge.38, f32[4,128,128]{2,1,0:T(8,128)S(1)} %fusion.49, f32[4,128,128]{2,1,0:T(8,128)S(1)} %fusion.46, ...), kind=kOutput, calls=%fused_computation.13 | convolution fusion | flops 906952704 | bytes 3538945 | tf_op jit(solution)/shard_map/hid,hjd->hij/dot_general | solution.py:34
  210.7 2.5 select_dynamic-update-slice_fusion
  213.2 5.3 %multiply_reduce_fusion = f32[4,384]{1,0:T(4,128)S(1)} fusion(f32[4,384,1920]{1,2,0:T(8,128)} %select_dynamic-update-slice_fusion), kind=kLoop, calls=%fused_computation.1 | loop fusion | flops 5896704 | bytes 11802624 | tf_op jit(solution)/shard_map/reduce_max | solution.py:99
  218.5 2.4 copy-done.1
  222.9 2.4 fusion.19
  226.5 25.0 %all_to_all.5 = bf16[4,384,512]{2,1,0:T(8,128)(2,1)} all-to-all(bf16[4,384,512]{2,1,0:T(8,128)(2,1)S(1)} %bitcast.147), channel_id=1, replica_groups=mesh['seq'=64,'head'=4] {'head'}, dimensions={0} | all-to-all | bytes 3145728 | tf_op jit(solution)/shard_map/all_to_all | solution.py:29
  251.5 2.5 reduce_sum.32
  (115 shorter events, 42.4 us)
Async XLA Ops:
  0.0 225.3 %copy-start = (bf16[512,2048]{1,0:T(8,128)(2,1)S(1)}, bf16[512,2048]{1,0:T(8,128)(2,1)}, u32[]{:S(2)}) copy-start(bf16[512,2048]{1,0:T(8,128)(2,1)} %param.11) | copy-start | bytes 6291460
  0.0 3.9 %copy-start.24 = (f32[4,384]{1,0:T(4,128)S(1)}, f32[4,384]{1,0:T(4,128)}, u32[]{:S(2)}) copy-start(f32[4,384]{1,0:T(4,128)} %param.10) | copy-start | bytes 18436
  0.0 153.4 %copy-start.16 = (f32[128,128]{1,0:T(8,128)}, f32[128,128]{1,0:T(8,128)S(1)}, u32[]{:S(2)}) copy-start(f32[128,128]{1,0:T(8,128)S(1)} %fusion.59) | copy-start | bytes 196612
  129.0 3.3 %copy-start.2 = (f32[12,128,128]{1,2,0:T(8,128)}, f32[12,128,128]{1,2,0:T(8,128)S(1)}, u32[]{:S(2)}) copy-start(f32[12,128,128]{1,2,0:T(8,128)S(1)} %fusion.23) | copy-start | bytes 2359300
  130.4 3.3 %copy-start.6 = (f32[4,3,128,128]{3,2,1,0:T(8,128)}, f32[4,3,128,128]{3,2,1,0:T(8,128)S(1)}, u32[]{:S(2)}) copy-start(f32[4,3,128,128]{3,2,1,0:T(8,128)S(1)} %fusion.31) | copy-start | bytes 2359300
  132.2 4.0 %copy-start.22 = (bf16[384,512]{1,0:T(8,128)(2,1)S(1)}, bf16[384,512]{1,0:T(8,128)(2,1)}, u32[]{:S(2)}) copy-start(bf16[384,512]{1,0:T(8,128)(2,1)} %param.7) | copy-start | bytes 1179652
  141.1 3.2 %copy-start.12 = (f32[4,3,128,128]{3,2,0,1:T(8,128)}, f32[4,3,128,128]{3,2,0,1:T(8,128)S(1)}, u32[]{:S(2)}) copy-start(f32[4,3,128,128]{3,2,0,1:T(8,128)S(1)} %convolution_subtract_fusion.1) | copy-start | bytes 2359300
  144.3 34.1 %collective-permute-start = (bf16[4,384,128]{2,1,0:T(8,128)(2,1)}, bf16[4,384,128]{2,1,0:T(8,128)(2,1)}, u32[]{:S(2)}, u32[]{:S(2)}) collective-permute-start(bf16[4,384,128]{2,1,0:T(8,128)(2,1)} %fusion.43), channel_id=1, source_target_pairs={{0,4},{4,8},{8,12},{12,16},{16,20},{20,24},{24,28},{28,32},{32,36}... | collective-permute-start | bytes 1179656 | tf_op jit(solution)/shard_map/ppermute | solution.py:18
  151.1 8.6 %copy-start.23 = (bf16[384,512]{1,0:T(8,128)(2,1)S(1)}, bf16[384,512]{1,0:T(8,128)(2,1)}, u32[]{:S(2)}) copy-start(bf16[384,512]{1,0:T(8,128)(2,1)} %param.6) | copy-start | bytes 1179652
  151.1 32.6 %collective-permute-start.4 = (bf16[4,384,128]{1,2,0:T(8,128)(2,1)}, bf16[4,384,128]{1,2,0:T(8,128)(2,1)}, u32[]{:S(2)}, u32[]{:S(2)}) collective-permute-start(bf16[4,384,128]{1,2,0:T(8,128)(2,1)} %bitcast.157), channel_id=1, source_target_pairs={{0,4},{4,8},{8,12},{12,16},{16,20},{20,24},{24,28},{28,32},{32,36}... | collective-permute-start | bytes 1179656 | tf_op jit(solution)/shard_map/ppermute | solution.py:18
  160.6 7.1 %copy-start.11 = (f32[4,384,128]{2,1,0:T(8,128)S(1)}, f32[4,384,128]{2,1,0:T(8,128)}, u32[]{:S(2)}) copy-start(f32[4,384,128]{2,1,0:T(8,128)} %copy-done.10) | copy-start | bytes 2359300
  162.7 6.5 %copy-start.5 = (f32[4,3,128,128]{3,2,1,0:T(8,128)S(1)}, f32[4,3,128,128]{3,2,1,0:T(8,128)}, u32[]{:S(2)}) copy-start(f32[4,3,128,128]{3,2,1,0:T(8,128)} %copy-done.3) | copy-start | bytes 2359300
  162.7 6.4 %copy-start.18 = (f32[4,128,128]{2,1,0:T(8,128)S(1)}, f32[4,128,128]{2,1,0:T(8,128)}, u32[]{:S(2)}) copy-start(f32[4,128,128]{2,1,0:T(8,128)} %fusion.50) | copy-start | bytes 786436
  165.2 5.5 %copy-start.9 = (f32[4,3,128,128]{3,2,1,0:T(8,128)}, f32[4,3,128,128]{3,2,1,0:T(8,128)S(1)}, u32[]{:S(2)}) copy-start(f32[4,3,128,128]{3,2,1,0:T(8,128)S(1)} %convolution_subtract_fusion.3) | copy-start | bytes 2359300
  167.8 3.0 %copy-start.14 = (f32[4,3,128,128]{2,3,1,0:T(8,128)S(1)}, f32[4,3,128,128]{2,3,1,0:T(8,128)}, u32[]{:S(2)}) copy-start(f32[4,3,128,128]{2,3,1,0:T(8,128)} %fusion.33) | copy-start | bytes 2359300
  173.4 3.3 %copy-start.19 = (f32[4,128,256]{1,2,0:T(8,128)S(1)}, f32[4,128,256]{1,2,0:T(8,128)}, u32[]{:S(2)}) copy-start(f32[4,128,256]{1,2,0:T(8,128)} %fusion.35) | copy-start | bytes 1572868
  175.3 2.9 %copy-start.20 = (bf16[384,512]{0,1:T(8,128)(2,1)S(1)}, bf16[384,512]{0,1:T(8,128)(2,1)}, u32[]{:S(2)}) copy-start(bf16[384,512]{0,1:T(8,128)(2,1)} %copy.98) | copy-start | bytes 1179652
  179.8 10.5 %collective-permute-start.1 = (bf16[4,384,128]{2,1,0:T(8,128)(2,1)S(1)}, bf16[4,384,128]{2,1,0:T(8,128)(2,1)S(1)}, u32[]{:S(2)}, u32[]{:S(2)}) collective-permute-start(bf16[4,384,128]{2,1,0:T(8,128)(2,1)S(1)} %convolution_convert_fusion.3), channel_id=1, source_target_pairs={{0,4},{4,8},{8,12},{12,16},{16,20},{20,24},{24,28},{28,32},{32,36}... | collective-permute-start | bytes 1179656 | tf_op jit(solution)/shard_map/ppermute | solution.py:18
  183.8 10.9 %collective-permute-start.5 = (bf16[4,384,128]{1,2,0:T(8,128)(2,1)}, bf16[4,384,128]{1,2,0:T(8,128)(2,1)S(1)}, u32[]{:S(2)}, u32[]{:S(2)}) collective-permute-start(bf16[4,384,128]{1,2,0:T(8,128)(2,1)} %collective-permute-done.4), channel_id=1, source_target_pairs={{0,4},{4,8},{8,12},{12,16},{16,20},{20,24},{24,28},{28,32},{32,36}... | collective-permute-start | bytes 1179656 | tf_op jit(solution)/shard_map/ppermute | solution.py:18
  190.8 9.1 %collective-permute-start.2 = (bf16[4,384,128]{2,1,0:T(8,128)(2,1)S(1)}, bf16[4,384,128]{2,1,0:T(8,128)(2,1)S(1)}, u32[]{:S(2)}, u32[]{:S(2)}) collective-permute-start(bf16[4,384,128]{2,1,0:T(8,128)(2,1)S(1)} %convolution_convert_fusion.2), channel_id=1, source_target_pairs={{0,4},{4,8},{8,12},{12,16},{16,20},{20,24},{24,28},{28,32},{32,36}... | collective-permute-start | bytes 1179656 | tf_op jit(solution)/shard_map/ppermute | solution.py:18
  194.7 10.4 %collective-permute-start.6 = (bf16[4,384,128]{1,2,0:T(8,128)(2,1)S(1)}, bf16[4,384,128]{1,2,0:T(8,128)(2,1)S(1)}, u32[]{:S(2)}, u32[]{:S(2)}) collective-permute-start(bf16[4,384,128]{1,2,0:T(8,128)(2,1)S(1)} %collective-permute-done.5), channel_id=1, source_target_pairs={{0,4},{4,8},{8,12},{12,16},{16,20},{20,24},{24,28},{28,32},{32,36}... | collective-permute-start | bytes 1179656 | tf_op jit(solution)/shard_map/ppermute | solution.py:18
  200.4 10.2 %collective-permute-start.3 = (bf16[4,384,128]{2,1,0:T(8,128)(2,1)S(1)}, bf16[4,384,128]{2,1,0:T(8,128)(2,1)S(1)}, u32[]{:S(2)}, u32[]{:S(2)}) collective-permute-start(bf16[4,384,128]{2,1,0:T(8,128)(2,1)S(1)} %convolution_convert_fusion.1), channel_id=1, source_target_pairs={{0,4},{4,8},{8,12},{12,16},{16,20},{20,24},{24,28},{28,32},{32,36}... | collective-permute-start | bytes 1179656 | tf_op jit(solution)/shard_map/ppermute | solution.py:18
  205.2 17.6 %collective-permute-start.7 = (bf16[4,384,128]{1,2,0:T(8,128)(2,1)S(1)}, bf16[4,384,128]{1,2,0:T(8,128)(2,1)S(1)}, u32[]{:S(2)}, u32[]{:S(2)}) collective-permute-start(bf16[4,384,128]{1,2,0:T(8,128)(2,1)S(1)} %collective-permute-done.6), channel_id=1, source_target_pairs={{0,4},{4,8},{8,12},{12,16},{16,20},{20,24},{24,28},{28,32},{32,36}... | collective-permute-start | bytes 1179656 | tf_op jit(solution)/shard_map/ppermute | solution.py:18
  213.2 7.7 %copy-start.1 = (f32[4,384,1920]{1,2,0:T(8,128)S(1)}, f32[4,384,1920]{1,2,0:T(8,128)}, u32[]{:S(2)}) copy-start(f32[4,384,1920]{1,2,0:T(8,128)} %select_dynamic-update-slice_fusion) | copy-start | bytes 35389444
  (9 other events, 17.9 us)
where the time goes:
time: 259 us; the launch traced here: 254 us
  other arithmetic  134 us (52%)
  matrix products  53 us (20%)
  starting transfers between devices  27 us (10%)
  blocking collectives  25 us (10%)
  local copies, waits for them, and re-layouts  14.3 us (6%)
    another operation x4, other arithmetic, solve_unit(): jax.scipy.linalg.solve_triangular(matrix, identity_run, lower=True, unit_...  121 us
    dot_general x29, matrix products, product(): return jnp.einsum(pattern, first_op, second_op, precision=highest)  47 us
    ppermute x8, starting transfers between devices, shifted(): return lax.ppermute(block, axis, route)  27 us
    all_to_all x1, blocking collectives, summed_on_arrival(): tiles = lax.all_to_all(cut_along(shard, dim, count), axis, 0, 0, tiled=True)  25 us
    unnamed x57, local copies, waits for them, and re-layouts  8.84 us
    reduce_max x1, other arithmetic, attend(): maxima = jnp.max(scores, axis=2, keepdims=True)  5.29 us
  transfers between devices with their start and end apart: 8, of which 0 were waited for; matrix products, arithmetic and copies ran while one was open for 19% of the time, Pallas kernels for 0%

commit v1 on v0

v1 whole, which is shorter than its diff:
```python
import functools
import math

import jax
import jax.numpy as jnp
from jax import lax
from jax.experimental import pallas as pl
from jax.experimental.pallas import tpu as pltpu
from jax.sharding import PartitionSpec as P

F32, BF16 = jnp.float32, jnp.bfloat16
MESH = pl.DeviceIdType.MESH
SUB = 128
SCALE = math.log2(math.e) / math.sqrt(128.0)
ABSENT = -1e30
GROUP = 2

NN = (((1,), (0,)), ((), ()))
NT = (((1,), (1,)), ((), ()))
TN = (((0,), (0,)), ((), ()))


def dot1(a, b, dims=NN):
    return lax.dot_general(a, b, dims, preferred_element_type=F32)


def halves(x):
    high = x.astype(BF16)
    return high, (x - high.astype(F32)).astype(BF16)


def dot3(a, b, dims=NN):
    ah, al = halves(a)
    bh, bl = halves(b)
    k = dims[0][1][0]
    both = jnp.concatenate([bh, bl], 1 - k)
    r = dot1(jnp.concatenate([ah, al], 1), jnp.concatenate([both, both], k), dims)
    half = r.shape[1] // 2
    return r[:, :half] + r[:, half:]


def twice(a, b, dims=NN):
    k = dims[0][1][0]
    return dot1(jnp.concatenate(halves(a), 1), jnp.concatenate([b, b], k), dims)


def each(f, *lists):
    return [f(*t) for t in zip(*lists)]


def grid_ids():
    return (
        lax.broadcasted_iota(jnp.int32, (SUB, SUB), 0),
        lax.broadcasted_iota(jnp.int32, (SUB, SUB), 1),
    )


def local_heads(q, k, w, beta):
    runs = q[0].shape[0] // SUB
    row, col = grid_ids()
    eye = row == col

    def cut(x):
        return [a[r * SUB : (r + 1) * SUB] for a in x for r in range(runs)]

    qr, kr, wr = cut(q), cut(k), cut(w)
    br = [b[:, r * SUB : (r + 1) * SUB] for b in beta for r in range(runs)]
    t = each(lambda a, b, c: dot1(jnp.concatenate([c, a, b], 0), c, NT), qr, kr, wr)
    g = [x[:SUB] for x in t]
    a = [jnp.where(row >= col, x[SUB : 2 * SUB], 0.0) for x in t]
    c = [jnp.where(row < col, x[2 * SUB :], 0.0) for x in t]
    d_row = each(lambda x, b: b / (jnp.sum(jnp.where(eye, x, 0.0), 0, keepdims=True) + 1e-6), g, br)
    d_col = [jnp.sum(jnp.where(eye, x, 0.0), 1, keepdims=True) for x in d_row]

    def corner(b):
        return ((row // (2 * b)) == (col // (2 * b))) & ((row & b) != 0) & ((col & b) == 0)

    first = corner(1)
    inv = each(
        lambda x, dr, dc: jnp.where(eye, dr, jnp.where(first, -(x * dc) * dr, 0.0)), g, d_row, d_col
    )
    for b in (2, 4, 8, 16, 32, 64):
        mask = corner(b)
        m = [jnp.where(mask, x, 0.0) for x in g]
        z = each(lambda x, y: dot3(x, y), inv, m)
        inv = each(lambda x, y: x - dot3(y, x), inv, z)
    f = each(lambda x, y: dot3(x, y, NT), c, inv)
    ke = each(lambda x, y, d: x.astype(F32) - twice(y, d), kr, f, wr)
    y = each(lambda x, d: twice(x, d), inv, wr)
    unit = eye.astype(F32)

    def run_map(d, x):
        return unit - dot1(jnp.concatenate([d, d], 0), jnp.concatenate(halves(x), 0), TN)

    p = each(run_map, wr, y)
    qs = each(lambda x, e, z: (x.astype(F32) - dot3(e, z)) * SCALE, qr, a, y)
    ins = each(lambda x, z, e, h: (dot1(x, z, NT) - dot3(e, h, NT)) * SCALE, qr, kr, a, f)
    ins = [jnp.where(row >= col, x, -jnp.inf) for x in ins]
    out = []
    for i in range(len(q)):
        e1, e2, e3 = ke[3 * i : 3 * i + 3]
        p1, p2, p3 = p[3 * i : 3 * i + 3]
        q1, q2, q3 = qs[3 * i : 3 * i + 3]
        c2 = jnp.concatenate([dot3(e1, p2, NT), e2], 0)
        kt = jnp.concatenate([dot3(c2, p3, NT), e3], 0).astype(BF16)
        prefix = dot3(p2, p1)
        qt = jnp.concatenate([q1, dot3(q2, p1), dot3(q3, prefix)], 0)
        s2 = jnp.concatenate([dot3(q2, e1, NT), ins[3 * i + 1]], 1)
        s3 = jnp.concatenate([dot3(q3, c2, NT), ins[3 * i + 2]], 1)
        out.append((kt, qt, dot3(p3, prefix), [ins[3 * i], s2, s3]))
    return out


def wide(x, count=1):
    x = jnp.broadcast_to(x, (SUB, SUB))
    return x if count == 1 else jnp.concatenate([x] * count, 1)


def kernel(
    q, k, v, w, beta, wt, out,
    kbuf, kmid, qbuf, qmid, vbuf, pbuf, qn, oacc, mst, lst, osend, ofar, lsend, lfar, abuf, wbuf, wrel,
    send, recv, own,
):
    n_seq, n_head = lax.axis_size("seq"), lax.axis_size("head")
    s, h = lax.axis_index("seq"), lax.axis_index("head")
    nxt, prv = lax.rem(s + 1, n_seq), lax.rem(s + n_seq - 1, n_seq)
    nxt2, prv2 = lax.rem(s + 2, n_seq), lax.rem(s + n_seq - 2, n_seq)
    up, down, across = lax.rem(h + 1, n_head), lax.rem(h + n_head - 1, n_head), lax.rem(h + 2, n_head)
    length = q.shape[0]
    runs = length // SUB
    heads = q.shape[1] // SUB
    groups = heads // GROUP
    width = out.shape[1]
    half = length // 2
    depth_half = wt.shape[0] // 2
    row, col = grid_ids()
    eye = row == col

    barrier = pltpu.get_barrier_semaphore()
    for device in ({"seq": prv}, {"seq": nxt}, {"seq": prv2}, {"head": up}, {"head": down}):
        pl.semaphore_signal(barrier, inc=1, device_id=device, device_id_type=MESH)
    pl.semaphore_wait(barrier, 5)

    def remote(src, dst, i, device):
        return pltpu.make_async_remote_copy(
            src_ref=src, dst_ref=dst, send_sem=send.at[i], recv_sem=recv.at[i],
            device_id=device, device_id_type=MESH,
        )

    def heads_of(g):
        return pl.ds(g * GROUP, GROUP)

    def columns(c):
        return pl.ds(pl.multiple_of(c * width, width), width)

    lo, hi = pl.ds(0, depth_half), pl.ds(depth_half, depth_half)
    v_first = remote(v, vbuf.at[0], 0, {"seq": nxt})
    v_second = remote(vbuf.at[0], vbuf.at[1], 1, {"seq": nxt})
    w_up = remote(wt.at[:, columns(up)], wbuf.at[0], 2, {"head": up})
    w_down = remote(wt.at[:, columns(down)], wbuf.at[1], 3, {"head": down})
    w_rel_up = remote(wt.at[lo, columns(across)], wrel.at[0], 4, {"head": up})
    w_rel_down = remote(wt.at[hi, columns(across)], wrel.at[1], 5, {"head": down})
    w_far_up = remote(wrel.at[0], wbuf.at[2, lo], 6, {"head": up})
    w_far_down = remote(wrel.at[1], wbuf.at[2, hi], 7, {"head": down})

    def k_first(g):
        return remote(kbuf.at[0, heads_of(g)], kbuf.at[1, heads_of(g)], 8 + g, {"seq": nxt})

    def k_second(g):
        return remote(kmid.at[heads_of(g)], kbuf.at[2, heads_of(g)], 10 + g, {"seq": nxt})

    def q_first(g):
        return remote(qbuf.at[0, heads_of(g)], qbuf.at[1, heads_of(g)], 12 + g, {"seq": prv})

    def q_second(g):
        return remote(qmid.at[heads_of(g)], qbuf.at[2, heads_of(g)], 14 + g, {"seq": prv})

    def o_back(g):
        return remote(osend.at[heads_of(g)], ofar.at[heads_of(g)], 16 + g, {"seq": nxt2})

    def l_back(g):
        return remote(lsend.at[heads_of(g)], lfar.at[heads_of(g)], 18 + g, {"seq": nxt2})

    def a_up(g):
        return remote(abuf.at[0, heads_of(g)], abuf.at[1, heads_of(g)], 20 + g, {"head": up})

    def a_down(g):
        return remote(abuf.at[0, heads_of(g)], abuf.at[2, heads_of(g)], 22 + g, {"head": down})

    def a_far_up(g):
        part = pl.ds(0, half)
        return remote(abuf.at[1, heads_of(g), part], abuf.at[3, heads_of(g), part], 24 + g, {"head": up})

    def a_far_down(g):
        part = pl.ds(half, half)
        return remote(abuf.at[2, heads_of(g), part], abuf.at[3, heads_of(g), part], 26 + g, {"head": down})

    v_first.start()
    w_rel_up.start()
    w_rel_down.start()
    w_up.start()
    w_down.start()
    w_own = pltpu.make_async_copy(wt.at[:, columns(h)], wbuf.at[3], own)
    w_own.start()

    lanes = [pl.ds(x * SUB, SUB) for x in range(heads)]
    done = local_heads(
        [q[:, x] for x in lanes],
        [k[:, x] for x in lanes],
        [w[:, x] for x in lanes],
        [2.0 * jax.nn.sigmoid(beta[x : x + 1, :]) for x in range(heads)],
    )
    for x, (kt, qt, pb, _) in enumerate(done):
        kbuf[0, x] = kt
        qh, ql = halves(qt)
        qbuf[0, x] = qh
        qn[x, :, :SUB] = qh
        qn[x, :, SUB:] = ql
        ph, plow = halves(pb)
        pbuf[x, :, :SUB] = ph
        pbuf[x, :, SUB:] = plow
        if x % GROUP == GROUP - 1:
            k_first(x // GROUP).start()
            q_first(x // GROUP).start()
    v_first.wait_recv()
    v_second.start()
    w_rel_up.wait_recv()
    w_far_up.start()
    w_rel_down.wait_recv()
    w_far_down.start()

    for x, (_, _, _, scores) in enumerate(done):
        for r, sc in enumerate(scores):
            rows = pl.ds(r * SUB, SUB)
            top = jnp.max(sc, 1, keepdims=True)
            e = jnp.exp2(sc - top)
            mst[x, rows] = wide(top)
            lst[x, rows] = wide(jnp.sum(e, 1, keepdims=True))
            oacc[x, rows] = dot1(e.astype(BF16), v[: (r + 1) * SUB, lanes[x]])

    @pl.loop(0, groups)
    def _(g):
        k_first(g).wait_recv()
        for i in range(GROUP):
            x = g * GROUP + i
            kk = kbuf[1, x]
            kmid[x] = dot1(jnp.concatenate([kk, kk], 1), pbuf[x], NT).astype(BF16)
        k_second(g).start()
        q_first(g).wait_recv()
        for i in range(GROUP):
            x = g * GROUP + i
            qq = qbuf[1, x]
            pp = jnp.concatenate([pbuf[x, :, :SUB], pbuf[x, :, SUB:]], 0)
            qmid[x] = dot1(jnp.concatenate([qq, qq], 1), pp).astype(BF16)
        q_second(g).start()

    near = jnp.where(s >= 1, 0.0, ABSENT).astype(F32)
    beyond = jnp.where(s >= 2, 0.0, ABSENT).astype(F32)

    def window_scores(queries, keys):
        sc = dot1(queries, keys, NT)
        return jnp.concatenate([sc[:, :length] + near, sc[:, length:] + beyond], 1)

    def window_arrays(x):
        keys = jnp.concatenate([kbuf[1, x], kbuf[2, x]], 0)
        lane = pl.ds(pl.multiple_of(x * SUB, SUB), SUB)
        return jnp.concatenate([keys, keys], 1), jnp.concatenate([vbuf[0, :, lane], vbuf[1, :, lane]], 0)

    v_second.wait_recv()

    @pl.loop(0, groups)
    def _(g):
        k_second(g).wait_recv()
        q_second(g).wait_recv()
        for i in range(GROUP):
            x = g * GROUP + i
            qq = qbuf[2, x]
            pp = jnp.concatenate([pbuf[x, :, :SUB], pbuf[x, :, SUB:]], 0)
            moved = jnp.concatenate(halves(dot1(jnp.concatenate([qq, qq], 1), pp)), 1)
            keys, vals = window_arrays(x)
            for r in range(runs):
                rows = pl.ds(r * SUB, SUB)
                sc = window_scores(moved[r * SUB : (r + 1) * SUB], keys)
                top = jnp.max(sc, 1, keepdims=True)
                e = jnp.exp2(sc - top)
                total = jnp.sum(e, 1, keepdims=True)
                osend[x, rows] = (dot1(e.astype(BF16), vals) / total).astype(BF16)
                level = wide(top + jnp.log2(total))
                lsend[x, r : r + 1] = jnp.sum(jnp.where(eye, level, 0.0), 0, keepdims=True)
        o_back(g).start()
        l_back(g).start()

    @pl.loop(0, groups)
    def _(g):
        for i in range(GROUP):
            x = g * GROUP + i
            keys, vals = window_arrays(x)
            for r in range(runs):
                rows = pl.ds(r * SUB, SUB)
                sc = window_scores(qn[x, rows], keys)
                before = mst[x, rows]
                top = jnp.maximum(before, wide(jnp.max(sc, 1, keepdims=True)))
                e = jnp.exp2(sc - jnp.concatenate([top] * (2 * runs), 1))
                keep = jnp.exp2(before - top)
                mst[x, rows] = top
                lst[x, rows] = lst[x, rows] * keep + wide(jnp.sum(e, 1, keepdims=True))
                oacc[x, rows] = oacc[x, rows] * keep + dot1(e.astype(BF16), vals)

    @pl.loop(0, groups)
    def _(g):
        o_back(g).wait_recv()
        l_back(g).wait_recv()
        for i in range(GROUP):
            x = g * GROUP + i
            for r in range(runs):
                rows = pl.ds(r * SUB, SUB)
                level = jnp.where(s >= 3, lfar[x, r : r + 1], ABSENT)
                level = wide(jnp.sum(jnp.where(eye, level, 0.0), 1, keepdims=True))
                before = mst[x, rows]
                top = jnp.maximum(before, level)
                keep, other = jnp.exp2(before - top), jnp.exp2(level - top)
                total = lst[x, rows] * keep + other
                mix = oacc[x, rows] * keep + ofar[x, rows].astype(F32) * other
                abuf[0, x, rows] = (mix / total).astype(BF16)
        a_up(g).start()
        a_down(g).start()

    w_up.wait_recv()
    w_down.wait_recv()
    w_far_up.wait_recv()
    w_far_down.wait_recv()

    def project(slot, weight):
        joined = jnp.concatenate([abuf[slot, x] for x in range(heads)], 1)
        return dot1(joined, weight)

    @pl.loop(0, groups)
    def _(g):
        a_up(g).wait_recv()
        a_far_up(g).start()
        a_down(g).wait_recv()
        a_far_down(g).start()

    w_own.wait()
    total = project(1, wbuf[0]) + project(2, wbuf[1]) + project(0, wbuf[3])
    for g in range(groups):
        a_far_up(g).wait_recv()
        a_far_down(g).wait_recv()
    out[...] = (total + project(3, wbuf[2])).astype(BF16)
    for copy in (v_first, v_second, w_up, w_down, w_rel_up, w_rel_down, w_far_up, w_far_down):
        copy.wait_send()

    @pl.loop(0, groups)
    def _(g):
        for copy in (k_first, k_second, q_first, q_second, o_back, l_back, a_up, a_down, a_far_up, a_far_down):
            copy(g).wait_send()


def per_device(q, k, v, w, beta, wt):
    length, width = q.shape
    heads = width // SUB
    stat = pltpu.VMEM((heads, length, SUB), F32)
    rows = pltpu.VMEM((heads, length, SUB), BF16)

    def rows_of(count):
        return pltpu.VMEM((count, heads, length, SUB), BF16)

    scratch = [
        rows_of(3), rows, rows_of(3), rows,
        pltpu.VMEM((2, length, width), BF16),
        pltpu.VMEM((heads, SUB, 2 * SUB), BF16),
        pltpu.VMEM((heads, length, 2 * SUB), BF16),
        stat, stat, stat, rows, rows,
        pltpu.VMEM((heads, 8, SUB), F32),
        pltpu.VMEM((heads, 8, SUB), F32),
        rows_of(4),
        pltpu.VMEM((4, width, width), BF16),
        pltpu.VMEM((2, width // 2, width), BF16),
        pltpu.SemaphoreType.DMA((28,)),
        pltpu.SemaphoreType.DMA((28,)),
        pltpu.SemaphoreType.DMA,
    ]
    vmem = pl.BlockSpec(memory_space=pltpu.VMEM)
    return pl.pallas_call(
        kernel,
        out_shape=jax.ShapeDtypeStruct((length, width), BF16),
        in_specs=[vmem] * 5 + [pl.BlockSpec(memory_space=pl.ANY)],
        out_specs=vmem,
        scratch_shapes=scratch,
        compiler_params=pltpu.CompilerParams(
            collective_id=0, has_side_effects=True, vmem_limit_bytes=56 << 20
        ),
    )(q, k, v, w, beta, wt)


def solution(mesh):
    return jax.shard_map(
        per_device,
        mesh=mesh,
        in_specs=(P("seq", "head"),) * 4 + (P("head", "seq"), P("head", None)),
        out_specs=P("seq", "head"),
        check_vma=False,
    )
```

time: 259 us -> 57 us (0.22); the launches traced: 254 us -> 56.7 us
  other arithmetic: 134 us -> 0 us
  Pallas kernels: 0 us -> 54.9 us
  matrix products: 53 us -> 0 us
  starting transfers between devices: 27 us -> 0 us
  blocking collectives: 25 us -> 0 us
  local copies, waits for them, and re-layouts: 14.3 us -> 1.77 us
    another operation x4 -> x0, other arithmetic: 121 us -> none  [solve_unit(): jax.scipy.linalg.solve_triangular(matrix, identity_run, lower=True, unit_...]
    pallas_call x0 -> x1, Pallas kernels: none -> 54.9 us  [per_device(): pl.pallas_call(kernel, out_shape=jax.ShapeDtypeStruct((length, width), BF...]
    dot_general x31 -> x0, matrix products: 50.4 us -> none  [the longest x29 47 us: product(): return jnp.einsum(pattern, first_op, second_op, precision=highest)]
    ppermute x8 -> x0, starting transfers between devices: 27 us -> none  [shifted(): return lax.ppermute(block, axis, route)]
    all_to_all x1 -> x0, blocking collectives: 25 us -> none  [summed_on_arrival(): tiles = lax.all_to_all(cut_along(shard, dim, count), axis, 0, 0, tiled=True)]
    unnamed x57 -> x1, local copies, waits for them, and re-layouts: 8.84 us -> 1.77 us
    reduce_max x1 -> x0, other arithmetic: 5.29 us -> none  [attend(): maxima = jnp.max(scores, axis=2, keepdims=True)]
    reduce_sum x3 -> x0, other arithmetic: 4.51 us -> none  [the longest x1 2.5 us: summed_on_arrival(): return jnp.sum(tiles.astype(jnp.float32), axis=0)]
  transfers between devices with their start and end apart: 8 -> 0, of which waited for: 0 -> 0; matrix products, arithmetic and copies ran while one was open for 19% -> 0% of each run, Pallas kernels for 0% -> 0%
where the time goes in v1:
time: 57 us; the launch traced here: 56.7 us
  Pallas kernels  54.9 us (96%)
  local copies, waits for them, and re-layouts  1.77 us (3%)
    pallas_call x1, Pallas kernels, per_device(): pl.pallas_call(kernel, out_shape=jax.ShapeDtypeStruct((length, width), BF...  54.9 us
    unnamed x1, local copies, waits for them, and re-layouts  1.77 us

profile of v1, /device:TPU:1, one launch (start us, length us, event | category | flops | bytes accessed | tf_op | source)
XLA Modules:
  0.0 56.7 jit_solution(9813278180882608724)
XLA Ops:
  0.0 54.9 %shard_map.64 = bf16[384,512]{1,0:T(8,128)(2,1)} custom-call(bf16[384,512]{1,0:T(8,128)(2,1)} %q.1, bf16[384,512]{1,0:T(8,128)(2,1)} %k.1, bf16[384,512]{1,0:T(8,128)(2,1)} %v.1, bf16[384,512]{1,0:T(8,128)(2,1)} %w.1, f32[4,384]{1,0:T(4,128)} %beta.1, bf16[512,2048]{1,0:T(8,128)(2,1)} %wt.1), custom_call_target="tpu_custom_call" | custom-call | tf_op jit(solution)/shard_map/pallas_call | solution.py:384
  54.9 1.8 %copy.8 = bf16[384,512]{1,0:T(8,128)(2,1)} copy(bf16[384,512]{1,0:T(8,128)(2,1)} %shard_map.64) | data formatting | bytes 786432

commit v2 on v1

v2 whole, which is shorter than its diff:
```python
import functools
import math

import jax
import jax.numpy as jnp
from jax import lax
from jax.experimental import pallas as pl
from jax.experimental.pallas import tpu as pltpu
from jax.sharding import PartitionSpec as P

F32, BF16 = jnp.float32, jnp.bfloat16
MESH = pl.DeviceIdType.MESH
SUB = 128
SCALE = math.log2(math.e) / math.sqrt(128.0)
ABSENT = -1e30
GROUP = 1
BATCH = 2

NN = (((1,), (0,)), ((), ()))
NT = (((1,), (1,)), ((), ()))
TN = (((0,), (0,)), ((), ()))


def dot1(a, b, dims=NN):
    return lax.dot_general(a, b, dims, preferred_element_type=F32)


def halves(x):
    high = x.astype(BF16)
    return high, (x - high.astype(F32)).astype(BF16)


def dot3(a, b, dims=NN):
    ah, al = halves(a)
    bh, bl = halves(b)
    k = dims[0][1][0]
    both = jnp.concatenate([bh, bl], 1 - k)
    r = dot1(jnp.concatenate([ah, al], 1), jnp.concatenate([both, both], k), dims)
    half = r.shape[1] // 2
    return r[:, :half] + r[:, half:]


def twice(a, b, dims=NN):
    k = dims[0][1][0]
    return dot1(jnp.concatenate(halves(a), 1), jnp.concatenate([b, b], k), dims)


def each(f, *lists):
    return [f(*t) for t in zip(*lists)]


def grid_ids():
    return (
        lax.broadcasted_iota(jnp.int32, (SUB, SUB), 0),
        lax.broadcasted_iota(jnp.int32, (SUB, SUB), 1),
    )


def local_heads(q, k, w, beta):
    runs = q[0].shape[0] // SUB
    row, col = grid_ids()
    eye = row == col

    def cut(x):
        return [a[r * SUB : (r + 1) * SUB] for a in x for r in range(runs)]

    qr, kr, wr = cut(q), cut(k), cut(w)
    br = [b[:, r * SUB : (r + 1) * SUB] for b in beta for r in range(runs)]
    t = each(lambda a, b, c: dot1(jnp.concatenate([c, a, b], 0), c, NT), qr, kr, wr)
    g = [x[:SUB] for x in t]
    a = [jnp.where(row >= col, x[SUB : 2 * SUB], 0.0) for x in t]
    c = [jnp.where(row < col, x[2 * SUB :], 0.0) for x in t]
    d_row = each(lambda x, b: b / (jnp.sum(jnp.where(eye, x, 0.0), 0, keepdims=True) + 1e-6), g, br)
    d_col = [jnp.sum(jnp.where(eye, x, 0.0), 1, keepdims=True) for x in d_row]

    def corner(b):
        return ((row // (2 * b)) == (col // (2 * b))) & ((row & b) != 0) & ((col & b) == 0)

    first = corner(1)
    inv = each(
        lambda x, dr, dc: jnp.where(eye, dr, jnp.where(first, -(x * dc) * dr, 0.0)), g, d_row, d_col
    )
    for b in (2, 4, 8, 16, 32, 64):
        mask = corner(b)
        m = [jnp.where(mask, x, 0.0) for x in g]
        z = each(lambda x, y: dot3(x, y), inv, m)
        inv = each(lambda x, y: x - dot3(y, x), inv, z)
    f = each(lambda x, y: dot3(x, y, NT), c, inv)
    ke = each(lambda x, y, d: x.astype(F32) - twice(y, d), kr, f, wr)
    y = each(lambda x, d: twice(x, d), inv, wr)
    unit = eye.astype(F32)

    def run_map(d, x):
        return unit - dot1(jnp.concatenate([d, d], 0), jnp.concatenate(halves(x), 0), TN)

    p = each(run_map, wr, y)
    qs = each(lambda x, e, z: (x.astype(F32) - dot3(e, z)) * SCALE, qr, a, y)
    ins = each(lambda x, z, e, h: (dot1(x, z, NT) - dot3(e, h, NT)) * SCALE, qr, kr, a, f)
    ins = [jnp.where(row >= col, x, -jnp.inf) for x in ins]
    out = []
    for i in range(len(q)):
        e1, e2, e3 = ke[3 * i : 3 * i + 3]
        p1, p2, p3 = p[3 * i : 3 * i + 3]
        q1, q2, q3 = qs[3 * i : 3 * i + 3]
        c2 = jnp.concatenate([dot3(e1, p2, NT), e2], 0)
        kt = jnp.concatenate([dot3(c2, p3, NT), e3], 0).astype(BF16)
        prefix = dot3(p2, p1)
        qt = jnp.concatenate([q1, dot3(q2, p1), dot3(q3, prefix)], 0)
        s2 = jnp.concatenate([dot3(q2, e1, NT), ins[3 * i + 1]], 1)
        s3 = jnp.concatenate([dot3(q3, c2, NT), ins[3 * i + 2]], 1)
        out.append((kt, qt, dot3(p3, prefix), [ins[3 * i], s2, s3]))
    return out


def wide(x, count=1):
    x = jnp.broadcast_to(x, (SUB, SUB))
    return x if count == 1 else jnp.concatenate([x] * count, 1)


def kernel(
    q_in, k_in, v_in, w_in, beta, wt, out,
    q, k, v, w, kbuf, kmid, qbuf, qmid, vbuf, pbuf, qn, oacc, mst, lst, osend, ofar, lsend, lfar, abuf, wbuf, wrel,
    acc, send, recv, own,
):
    n_seq, n_head = lax.axis_size("seq"), lax.axis_size("head")
    s, h = lax.axis_index("seq"), lax.axis_index("head")
    nxt, prv = lax.rem(s + 1, n_seq), lax.rem(s + n_seq - 1, n_seq)
    nxt2, prv2 = lax.rem(s + 2, n_seq), lax.rem(s + n_seq - 2, n_seq)
    up, down, across = lax.rem(h + 1, n_head), lax.rem(h + n_head - 1, n_head), lax.rem(h + 2, n_head)
    even = lax.rem(s, 2) == 0
    length = q.shape[0]
    runs = length // SUB
    heads = q.shape[1] // SUB
    groups = heads // GROUP
    width = out.shape[1]
    half = length // 2
    depth_half = wt.shape[0] // 2
    row, col = grid_ids()
    eye = row == col
    lanes = [pl.ds(x * SUB, SUB) for x in range(heads)]

    loads = [
        pltpu.make_async_copy(src, dst, own.at[i])
        for i, (src, dst) in enumerate(((w_in, w), (k_in, k), (q_in, q), (v_in, v)))
    ]
    for copy in loads:
        copy.start()

    barrier = pltpu.get_barrier_semaphore()
    for device in ({"seq": prv}, {"seq": nxt}, {"seq": prv2}, {"head": up}, {"head": down}):
        pl.semaphore_signal(barrier, inc=1, device_id=device, device_id_type=MESH)
    pl.semaphore_wait(barrier, 5)

    def remote(src, dst, i, device, sent=None):
        return pltpu.make_async_remote_copy(
            src_ref=src, dst_ref=dst, send_sem=send.at[i if sent is None else sent], recv_sem=recv.at[i],
            device_id=device, device_id_type=MESH,
        )

    def heads_of(g):
        return pl.ds(g * GROUP, GROUP)

    def columns(c):
        return pl.ds(pl.multiple_of(c * width, width), width)

    core = lax.rem(s, 2)
    twin = s + 1 - 2 * core
    part = depth_half // 2

    def rows_at(start, size):
        return pl.ds(pl.multiple_of(start, part), size)

    mine = rows_at(core * depth_half, depth_half)
    lo, hi = rows_at(core * depth_half, part), rows_at(core * depth_half + part, part)
    v_first = remote(v_in, vbuf.at[0], 0, {"seq": nxt})
    v_direct = remote(v_in, vbuf.at[1], 1, {"seq": nxt2}, 8 + 10 * groups)
    v_passed = remote(vbuf.at[0], vbuf.at[1], 1, {"seq": nxt})
    w_up = remote(wt.at[mine, columns(up)], wbuf.at[0, mine], 2, {"head": up})
    w_down = remote(wt.at[mine, columns(down)], wbuf.at[1, mine], 3, {"head": down})
    w_rel_up = remote(wt.at[lo, columns(across)], wrel.at[0], 4, {"head": up})
    w_rel_down = remote(wt.at[hi, columns(across)], wrel.at[1], 5, {"head": down})
    w_far_up = remote(wrel.at[0], wbuf.at[2, lo], 6, {"head": up})
    w_far_down = remote(wrel.at[1], wbuf.at[2, hi], 7, {"head": down})
    w_twin = [
        remote(wbuf.at[i, mine], wbuf.at[i, mine], 9 + 10 * groups + i, {"seq": twin}) for i in range(3)
    ]
    w_own = pltpu.make_async_copy(wt.at[:, columns(h)], wbuf.at[3], own.at[4])

    def k_first(g):
        return remote(kbuf.at[0, heads_of(g)], kbuf.at[1, heads_of(g)], 8 + g, {"seq": nxt})

    def k_second(g):
        return remote(kmid.at[heads_of(g)], kbuf.at[2, heads_of(g)], 8 + groups + g, {"seq": nxt})

    def q_first(g):
        return remote(qbuf.at[0, heads_of(g)], qbuf.at[1, heads_of(g)], 8 + 2 * groups + g, {"seq": prv})

    def q_second(g):
        return remote(qmid.at[heads_of(g)], qbuf.at[2, heads_of(g)], 8 + 3 * groups + g, {"seq": prv})

    def o_back(g):
        return remote(osend.at[heads_of(g)], ofar.at[heads_of(g)], 8 + 4 * groups + g, {"seq": nxt2})

    def l_back(g):
        return remote(lsend.at[heads_of(g)], lfar.at[heads_of(g)], 8 + 5 * groups + g, {"seq": nxt2})

    def a_up(g):
        return remote(abuf.at[0, heads_of(g)], abuf.at[1, heads_of(g)], 8 + 6 * groups + g, {"head": up})

    def a_down(g):
        return remote(abuf.at[0, heads_of(g)], abuf.at[2, heads_of(g)], 8 + 7 * groups + g, {"head": down})

    def a_far_up(g):
        part = pl.ds(0, half)
        return remote(
            abuf.at[1, heads_of(g), part], abuf.at[3, heads_of(g), part], 8 + 8 * groups + g, {"head": up}
        )

    def a_far_down(g):
        part = pl.ds(half, half)
        return remote(
            abuf.at[2, heads_of(g), part], abuf.at[3, heads_of(g), part], 8 + 9 * groups + g, {"head": down}
        )

    v_first.start()

    @pl.when(even)
    def _():
        v_direct.start()

    w_rel_up.start()
    w_rel_down.start()
    w_up.start()
    w_down.start()
    w_own.start()
    for copy in loads:
        copy.wait()

    near = jnp.where(s >= 1, 0.0, ABSENT).astype(F32)
    beyond = jnp.where(s >= 2, 0.0, ABSENT).astype(F32)

    def local(b):
        span = range(b * BATCH, (b + 1) * BATCH)
        done = local_heads(
            [q[:, lanes[x]] for x in span],
            [k[:, lanes[x]] for x in span],
            [w[:, lanes[x]] for x in span],
            [2.0 * jax.nn.sigmoid(beta[x : x + 1, :]) for x in span],
        )
        for x, (kt, qt, pb, _) in zip(span, done):
            kbuf[0, x] = kt
            qh, ql = halves(qt)
            qbuf[0, x] = qh
            qn[x, :, :SUB] = qh
            qn[x, :, SUB:] = ql
            ph, plow = halves(pb)
            pbuf[x, :, :SUB] = ph
            pbuf[x, :, SUB:] = plow
        return [d[3] for d in done]

    def with_ones(vals):
        return jnp.concatenate([vals, jnp.ones_like(vals)], 1)

    def own_share(b, scores):
        for x, parts in zip(range(b * BATCH, (b + 1) * BATCH), scores):
            for r, sc in enumerate(parts):
                rows = pl.ds(r * SUB, SUB)
                top = jnp.max(sc, 1, keepdims=True)
                e = jnp.exp2(sc - top).astype(BF16)
                both = dot1(e, with_ones(v[: (r + 1) * SUB, lanes[x]]))
                mst[x, rows] = wide(top)
                oacc[x, rows] = both[:, :SUB]
                lst[x, rows] = both[:, SUB:]

    def through_block(x, rows):
        pp = jnp.concatenate([pbuf[x, :, :SUB], pbuf[x, :, SUB:]], 0)
        return dot1(jnp.concatenate([rows, rows], 1), pp)

    def pass_on(g):
        k_first(g).wait_recv()
        for x in range(g * GROUP, (g + 1) * GROUP):
            kk = kbuf[1, x]
            kmid[x] = dot1(jnp.concatenate([kk, kk], 1), pbuf[x], NT).astype(BF16)
        k_second(g).start()
        q_first(g).wait_recv()
        for x in range(g * GROUP, (g + 1) * GROUP):
            qmid[x] = through_block(x, qbuf[1, x]).astype(BF16)
        q_second(g).start()

    def window(x):
        keys = jnp.concatenate([kbuf[1, x], kbuf[2, x]], 0)
        vals = jnp.concatenate([vbuf[0, :, lanes[x]], vbuf[1, :, lanes[x]]], 0)
        return jnp.concatenate([keys, keys], 1), with_ones(vals)

    def far_share(g):
        k_second(g).wait_recv()
        q_second(g).wait_recv()
        for x in range(g * GROUP, (g + 1) * GROUP):
            moved = jnp.concatenate(halves(through_block(x, qbuf[2, x])), 1)
            keys, vals = window(x)
            scores = dot1(moved, keys, NT)
            tops, weights = [], []
            for r in range(runs):
                sc = scores[r * SUB : (r + 1) * SUB]
                m0 = jnp.max(sc[:, :length], 1, keepdims=True)
                m1 = jnp.max(sc[:, length:], 1, keepdims=True)
                top = jnp.maximum(m0 + near, m1 + beyond)
                s0, s1 = jnp.maximum(top - near, m0), jnp.maximum(top - beyond, m1)
                tops.append(top)
                weights.append(
                    jnp.exp2(jnp.concatenate([sc[:, :length] - s0, sc[:, length:] - s1], 1)).astype(BF16)
                )
            both = dot1(jnp.concatenate(weights, 0), vals)
            for r in range(runs):
                rows = slice(r * SUB, (r + 1) * SUB)
                total = both[rows, SUB:]
                osend[x, rows] = (both[rows, :SUB] / total).astype(BF16)
                level = wide(tops[r]) + jnp.log2(total)
                lsend[x, r : r + 1] = jnp.sum(jnp.where(eye, level, 0.0), 0, keepdims=True)
        o_back(g).start()
        l_back(g).start()

    def near_share(g):
        for x in range(g * GROUP, (g + 1) * GROUP):
            keys, vals = window(x)
            scores = dot1(qn[x], keys, NT)
            keeps, weights = [], []
            for r in range(runs):
                rows = slice(r * SUB, (r + 1) * SUB)
                sc = scores[rows]
                m0 = jnp.max(sc[:, :length], 1, keepdims=True) + near
                m1 = jnp.max(sc[:, length:], 1, keepdims=True) + beyond
                before = mst[x, rows]
                top = jnp.maximum(before, wide(jnp.maximum(m0, m1)))
                shift = jnp.concatenate([top - near] * runs + [top - beyond] * runs, 1)
                weights.append(jnp.exp2(sc - shift).astype(BF16))
                keeps.append(jnp.exp2(before - top))
                mst[x, rows] = top
            both = dot1(jnp.concatenate(weights, 0), vals)
            for r in range(runs):
                rows = slice(r * SUB, (r + 1) * SUB)
                oacc[x, rows] = oacc[x, rows] * keeps[r] + both[rows, :SUB]
                lst[x, rows] = lst[x, rows] * keeps[r] + both[rows, SUB:]

    def merge(g):
        o_back(g).wait_recv()
        l_back(g).wait_recv()
        for x in range(g * GROUP, (g + 1) * GROUP):
            for r in range(runs):
                rows = pl.ds(r * SUB, SUB)
                level = jnp.where(s >= 3, lfar[x, r : r + 1], ABSENT)
                level = wide(jnp.sum(jnp.where(eye, level, 0.0), 1, keepdims=True))
                before = mst[x, rows]
                top = jnp.maximum(before, level)
                keep, other = jnp.exp2(before - top), jnp.exp2(level - top)
                total = lst[x, rows] * keep + other
                mix = oacc[x, rows] * keep + ofar[x, rows].astype(F32) * other
                abuf[0, x, rows] = (mix / total).astype(BF16)
        a_up(g).start()
        a_down(g).start()

    def gather_on(g):
        a_up(g).wait_recv()
        a_far_up(g).start()
        a_down(g).wait_recv()
        a_far_down(g).start()

    own_slot, up_slot, down_slot, far_slot = (0, 3), (1, 0), (2, 1), (3, 2)

    def project(*terms):
        left = [abuf[slot[0], x] for slot, g in terms for x in range(g * GROUP, (g + 1) * GROUP)]
        right = [
            wbuf[slot[1], x * SUB : (x + 1) * SUB] for slot, g in terms for x in range(g * GROUP, (g + 1) * GROUP)
        ]
        return dot1(jnp.concatenate(left, 1), jnp.concatenate(right, 0))

    def set_out(*which):
        for g in which:
            k_first(g).start()
            q_first(g).start()

    scores = local(0)
    set_out(0, 1)
    scores_late = local(1)
    set_out(2, 3)
    v_first.wait_recv()

    @pl.when(even)
    def _():
        v_passed.start()

    w_rel_up.wait_recv()
    w_far_up.start()
    w_rel_down.wait_recv()
    w_far_down.start()
    pass_on(0)
    pass_on(1)
    own_share(0, scores)
    own_share(1, scores_late)
    pass_on(2)
    pass_on(3)
    v_passed.wait_recv()
    last = groups - 1
    far_share(0)
    near_share(0)
    far_share(1)
    near_share(1)
    far_share(2)
    merge(0)
    near_share(2)
    far_share(3)
    merge(1)
    gather_on(0)
    for i, copy in enumerate((w_up, w_down)):
        copy.wait_recv()
        w_twin[i].start()
    w_far_up.wait_recv()
    w_far_down.wait_recv()
    w_twin[2].start()
    near_share(3)
    merge(2)
    gather_on(1)
    merge(3)
    gather_on(2)
    for copy in w_twin:
        copy.wait_recv()
    w_own.wait()
    every = range(groups)
    acc[...] = project(*((own_slot, g) for g in every))
    gather_on(last)
    acc[...] += project(*((slot, g) for slot in (up_slot, down_slot) for g in every))
    for g in every:
        a_far_up(g).wait_recv()
        a_far_down(g).wait_recv()
    out[...] = (acc[...] + project(*((far_slot, g) for g in every))).astype(BF16)

    for copy in (v_first, w_up, w_down, w_rel_up, w_rel_down, w_far_up, w_far_down, *w_twin):
        copy.wait_send()

    @pl.when(even)
    def _():
        v_direct.wait_send()
        v_passed.wait_send()

    for g in range(groups):
        for copy in (k_first, k_second, q_first, q_second, o_back, l_back, a_up, a_down, a_far_up, a_far_down):
            copy(g).wait_send()


def per_device(q, k, v, w, beta, wt):
    length, width = q.shape
    heads = width // SUB
    stat = pltpu.VMEM((heads, length, SUB), F32)
    rows = pltpu.VMEM((heads, length, SUB), BF16)

    def rows_of(count):
        return pltpu.VMEM((count, heads, length, SUB), BF16)

    scratch = [
        *[pltpu.VMEM((length, width), BF16)] * 4,
        rows_of(3), rows, rows_of(3), rows,
        pltpu.VMEM((2, length, width), BF16),
        pltpu.VMEM((heads, SUB, 2 * SUB), BF16),
        pltpu.VMEM((heads, length, 2 * SUB), BF16),
        stat, stat, stat, rows, rows,
        pltpu.VMEM((heads, 8, SUB), F32),
        pltpu.VMEM((heads, 8, SUB), F32),
        rows_of(4),
        pltpu.VMEM((4, width, width), BF16),
        pltpu.VMEM((2, width // 4, width), BF16),
        pltpu.VMEM((length, width), F32),
        pltpu.SemaphoreType.DMA((12 + 10 * heads // GROUP,)),
        pltpu.SemaphoreType.DMA((12 + 10 * heads // GROUP,)),
        pltpu.SemaphoreType.DMA((5,)),
    ]
    vmem, hbm = pl.BlockSpec(memory_space=pltpu.VMEM), pl.BlockSpec(memory_space=pl.ANY)
    return pl.pallas_call(
        kernel,
        out_shape=jax.ShapeDtypeStruct((length, width), BF16),
        in_specs=[hbm] * 4 + [vmem, hbm],
        out_specs=vmem,
        scratch_shapes=scratch,
        compiler_params=pltpu.CompilerParams(
            collective_id=0, has_side_effects=True, vmem_limit_bytes=56 << 20
        ),
    )(q, k, v, w, beta, wt)


def solution(mesh):
    return jax.shard_map(
        per_device,
        mesh=mesh,
        in_specs=(P("seq", "head"),) * 4 + (P("head", "seq"), P("head", None)),
        out_specs=P("seq", "head"),
        check_vma=False,
    )
```

time: 57 us -> 53.8 us (0.944)
  Pallas kernels: 54.9 us -> 51.9 us
    pallas_call x1, Pallas kernels: 54.9 us -> 51.9 us  [per_device(): pl.pallas_call(kernel, out_shape=jax.ShapeDtypeStruct((length, width), BF...]
where the time goes in v2:
time: 53.8 us; the launch traced here: 53.6 us
  Pallas kernels  51.9 us (96%)
  local copies, waits for them, and re-layouts  1.77 us (3%)
    pallas_call x1, Pallas kernels, per_device(): pl.pallas_call(kernel, out_shape=jax.ShapeDtypeStruct((length, width), BF...  51.9 us
    unnamed x1, local copies, waits for them, and re-layouts  1.77 us

profile of v2, /device:TPU:1, one launch (start us, length us, event | category | flops | bytes accessed | tf_op | source)
XLA Modules:
  0.0 53.6 jit_solution(11511491659245974845)
XLA Ops:
  0.0 51.9 %shard_map.64 = bf16[384,512]{1,0:T(8,128)(2,1)} custom-call(bf16[384,512]{1,0:T(8,128)(2,1)} %q_in.1, bf16[384,512]{1,0:T(8,128)(2,1)} %k_in.1, bf16[384,512]{1,0:T(8,128)(2,1)} %v_in.1, bf16[384,512]{1,0:T(8,128)(2,1)} %w_in.1, f32[4,384]{1,0:T(4,128)} %beta.1, bf16[512,2048]{1,0:T(8,128)(2,1)} %wt.1), custom_call_target="tpu_custom_call" | custom-call | tf_op jit(solution)/shard_map/pallas_call | solution.py:477
  51.9 1.8 %copy.8 = bf16[384,512]{1,0:T(8,128)(2,1)} copy(bf16[384,512]{1,0:T(8,128)(2,1)} %shard_map.64) | data formatting | bytes 786432
